TPU v7x, 256 devices: a whole 4x4x8 slice. The times are simulated.
256 devices in a mesh: user: 32 (over z, x), item: 4 (over y), rep: 2 (over core).
Axes of the slice: x: 4, y: 4, z: 8, core: 2. Of those that a mesh axis runs over, the one named last changes fastest.
Arguments:
- item_factors: bfloat16 [131072, 256], P(('user', 'item'))
- user_factors: bfloat16 [4096, 256], P(('user', 'item', 'rep')), may hold values from -6 to 6
- strengths: bfloat16 [4096, 1024], P(('user', 'item', 'rep')), may hold values from 0.5 to 40
- requests: int32 [256, 128], P(('user', 'item', 'rep')), may hold values from -1 to 7, as said below
- user_slots: int32 [4096, 8], P(('user', 'item', 'rep')), may hold values from 0 to 127, as said below
Outputs:
- user_new: float32 [4096, 256], P(('user', 'item', 'rep'))
- item_partial: float32 [131072, 256], P(('user', 'item'))
Inputs may be any that keep to these rules, and one draw needn't show every extreme that they name: `requests`: entry [d, o] names the one tile of owner o that device d reads, or is -1; every row has at least 8 entries that are not -1. `user_slots`: each row holds 8 different owners o, each with requests[u // 16, o] >= 0.
All inputs are finite; a program needn't handle non-finite values.
Results may differ from a plain program's by a relative error of at most 0.0051.
Values may be sent and summed in bfloat16 or wider, within the bound.
No kernel may reach another device: no remote copies, remote signals or barrier semaphores. Data moves between devices by JAX's collectives and lax.ppermute only.
A program may use at most 64 MiB of HBM per device.

v0:
```python
import math
import jax
import jax.numpy as jnp
from jax import lax
from jax.sharding import PartitionSpec as P

TILE = 128
SLOTS_USER = 8
ITERS = 2
penalty = 1.0


def absorb(tiles, gram_matrix, start_rows, strengths, user_slots):
    users = start_rows.shape[0]
    owners = tiles.shape[0]
    factor_dim = tiles.shape[2]
    group = math.gcd(users, 16)
    count = users // group

    def one_group(inputs):
        begin_rows, weight_rows, slot_rows = inputs
        block = tiles[slot_rows].reshape(group, SLOTS_USER * TILE, factor_dim)
        weights = weight_rows.astype(jnp.float32)
        confidence = (1.0 + weights).astype(jnp.bfloat16)
        rhs = jnp.einsum("uj,ujr->ur", confidence, block, preferred_element_type=jnp.float32)

        def against(vectors):
            return jnp.einsum("ur,ujr->uj", vectors, block, preferred_element_type=jnp.float32)

        def operate(vectors):
            scaled = (weights * against(vectors.astype(jnp.bfloat16))).astype(jnp.bfloat16)
            gram_part = jnp.dot(vectors, gram_matrix, precision=lax.Precision.HIGHEST)
            back = jnp.einsum("uj,ujr->ur", scaled, block, preferred_element_type=jnp.float32)
            return gram_part + back + penalty * vectors

        solution = begin_rows.astype(jnp.float32)
        residual = rhs - operate(solution)
        direction = residual
        norm_now = jnp.sum(residual * residual, axis=1, keepdims=True)
        for sweep in range(ITERS):
            image = operate(direction)
            step_size = norm_now / jnp.sum(direction * image, axis=1, keepdims=True)
            solution = solution + step_size * direction
            residual = residual - step_size * image
            norm_next = jnp.sum(residual * residual, axis=1, keepdims=True)
            direction = residual + norm_next / norm_now * direction
            norm_now = norm_next
        solved_rounded = solution.astype(jnp.bfloat16)
        fitted = against(solved_rounded)
        coeffs = (confidence.astype(jnp.float32) - weights * fitted).astype(jnp.bfloat16)
        return (solution, coeffs, solved_rounded)

    solution, coeffs, solved_rounded = lax.map(
        one_group,
        (
            start_rows.reshape(count, group, factor_dim),
            strengths.reshape(count, group, SLOTS_USER * TILE),
            user_slots.reshape(count, group, SLOTS_USER),
        ),
    )
    solution = solution.reshape(users, factor_dim)
    solved_rounded = solved_rounded.reshape(users, factor_dim)
    coeffs = coeffs.reshape(users, SLOTS_USER, TILE)
    onehot = (user_slots[:, :, None] == jnp.arange(owners, dtype=jnp.int32)[None, None, :]).astype(
        jnp.bfloat16
    )
    spread_coeffs = jnp.einsum("uko,ukj->uoj", onehot, coeffs, preferred_element_type=jnp.float32)
    spread_coeffs = spread_coeffs.astype(jnp.bfloat16).reshape(users, owners * TILE)
    return (solution, spread_coeffs, solved_rounded)


def shards(item_factors, user_factors, strengths, requests, user_slots):
    owners = lax.axis_size(("user", "item"))
    tiles_here = item_factors.shape[0] // TILE
    factor_dim = item_factors.shape[1]
    own_tiles = item_factors.reshape(tiles_here, TILE, factor_dim)
    local_gram = jnp.dot(item_factors.T, item_factors, preferred_element_type=jnp.float32)
    gram_matrix = lax.psum(local_gram, ("user", "item"))
    asked_tiles = lax.all_to_all(
        requests.reshape(owners), ("user", "item"), split_axis=0, concat_axis=0, tiled=True
    )
    tile_range = jnp.arange(tiles_here, dtype=jnp.int32)
    pick_float = (asked_tiles[:, None] == tile_range[None, :]).astype(jnp.float32)
    reply_tiles = jnp.einsum(
        "st,tjr->sjr",
        pick_float.astype(jnp.bfloat16),
        own_tiles,
        preferred_element_type=jnp.float32,
    ).astype(jnp.bfloat16)
    fetched = lax.all_to_all(reply_tiles, ("user", "item"), split_axis=0, concat_axis=0, tiled=True)
    solution, coeffs, solved_rounded = absorb(
        fetched, gram_matrix, user_factors, strengths, user_slots
    )
    partial_value = lax.dot_general(
        coeffs, solved_rounded, (((0,), (0,)), ((), ())), preferred_element_type=jnp.float32
    )
    arrived = lax.all_to_all(
        partial_value.reshape(owners, TILE, factor_dim),
        ("user", "item"),
        split_axis=0,
        concat_axis=0,
        tiled=True,
    )
    owned_sums = jnp.einsum("st,sjr->tjr", pick_float, arrived, precision=lax.Precision.HIGHEST)
    item_sums = lax.psum(owned_sums, "rep")
    return (solution, item_sums.reshape(tiles_here * TILE, factor_dim))


def solution(mesh):
    return jax.shard_map(
        shards,
        mesh=mesh,
        in_specs=(
            P(("user", "item"), None),
            P(("user", "item", "rep"), None),
            P(("user", "item", "rep"), None),
            P(("user", "item", "rep"), None),
            P(("user", "item", "rep"), None),
        ),
        out_specs=(P(("user", "item", "rep"), None), P(("user", "item"), None)),
        check_vma=False,
    )
```

profile of v0, /device:TPU:1, one launch (start us, length us, event | category | flops | bytes accessed | tf_op | source)
XLA Modules:
  0.0 765.9 jit_solution(2870779633857930631)
XLA Ops:
  7.2 0.8 copy.23
  8.0 26.9 %all_to_all.19 = s32[128,1,1]{2,1,0:T(1,128)S(1)} all-to-all(s32[128,1,1]{2,1,0:T(1,128)S(1)} %copy.23), channel_id=1, replica_groups=mesh['user'=32,'item'=4,'rep'=2] {'user','item'}, dimensions={0} | all-to-all | bytes 1024 | tf_op jit(solution)/shard_map/all_to_all | solution.py:79
  34.9 2.3 reduce
  37.2 5.6 convolution_convert_fusion
  42.8 11.4 %copy.25 = bf16[128,128,256]{2,1,0:T(8,128)(2,1)} copy(bf16[128,128,256]{2,0,1:T(8,128)(2,1)} %convolution_convert_fusion) | data formatting | bytes 16777216 | tf_op jit(solution)/shard_map/convert_element_type | solution.py:89
  54.2 7.8 %all-to-all-start.1 = ((bf16[128,128,256]{2,1,0:T(8,128)(2,1)}), bf16[128,128,256]{2,1,0:T(8,128)(2,1)}, u32[]{:S(2)}, u32[]{:S(2)}) async-start(bf16[128,128,256]{2,1,0:T(8,128)(2,1)} %copy.25), calls=%async_computation.1 | async-start | bytes 16777216 | tf_op jit(solution)/shard_map/all_to_all | solution.py:90
  62.0 1.0 fusion.49
  63.3 0.1 reshape.68
  63.4 182.3 %all-to-all-done.1 = bf16[128,128,256]{2,1,0:T(8,128)(2,1)} async-done(((bf16[128,128,256]{2,1,0:T(8,128)(2,1)}), bf16[128,128,256]{2,1,0:T(8,128)(2,1)}, u32[]{:S(2)}, u32[]{:S(2)}) %all-to-all-start.1) | async-done | bytes 8388640 | tf_op jit(solution)/shard_map/all_to_all | solution.py:90
  245.7 10.0 %gather_fusion = bf16[128,128,256]{2,1,0:T(8,128)(2,1)} fusion(bf16[128,128,256]{2,1,0:T(8,128)(2,1)} %all-to-all-done.1, s32[1024]{0:T(1024)S(1)} %pad_clamp_fusion), kind=kCustom, calls=%fused_computation | custom fusion | bytes 16777728 | tf_op jit(solution)/shard_map/while/body/eval_jaxpr/gather | solution.py:22
  255.7 5.8 fusion.40
  261.6 1.2 fusion.25
  262.8 1.2 fusion.23
  264.0 44.8 %all-reduce.3.cloned.1.call-done = f32[256,256]{1,0:T(8,128)} async-done(((f32[256,256]{1,0:T(8,128)}), f32[256,256]{1,0:T(8,128)}) %all-reduce.3.cloned.1.call-update) | async-done | bytes 262160 | tf_op jit(solution)/shard_map/psum | solution.py:78
  308.7 1.2 fusion.7
  309.9 5.6 fusion.38
  315.6 4.7 fusion.21
  320.3 0.3 multiply_reduce_fusion.1
  320.7 0.2 multiply_reduce_fusion
  321.0 0.5 slice-done.1
  321.5 2.3 fusion.36
  323.8 1.2 fusion.19
  325.0 0.4 fusion.8
  325.4 0.7 convert_bitcast_fusion
  326.1 2.3 fusion.34
  328.4 0.6 convolution_convert_fusion.1
  328.9 8.1 %fusion.9 = f32[128,128,256]{2,1,0:T(8,128)} fusion(bf16[16,256,1]{1,0,2:T(8,128)(2,1)S(1)} %get-tuple-element.22, bf16[2,8,128,128]{3,2,1,0:T(8,128)(2,1)S(1)} %bitcast.102), kind=kOutput, calls=%fused_computation.16 | convolution fusion | flops 134217728 | bytes 17309696 | tf_op jit(solution)/shard_map/dot_general | solution.py:94
  337.1 367.3 %all_to_all.20 = f32[128,128,256]{2,1,0:T(8,128)S(1)} all-to-all(f32[128,128,256]{2,1,0:T(8,128)} %fusion.9), channel_id=1, replica_groups=mesh['user'=32,'item'=4,'rep'=2] {'user','item'}, dimensions={0} | all-to-all | bytes 33554432 | tf_op jit(solution)/shard_map/all_to_all | solution.py:97
  704.3 15.2 %fusion = f32[8,128,256]{2,0,1:T(8,128)S(1)} fusion(f32[128,128,256]{2,1,0:T(8,128)S(1)} %all_to_all.20, s32[128]{0:T(128)S(1)} %reduce), kind=kOutput, calls=%fused_computation.1 | convolution fusion | flops 402654208 | bytes 17826304 | tf_op jit(solution)/shard_map/st,sjr->tjr/dot_general | solution.py:104
  719.5 1.3 copy.31
  720.8 35.6 %all-reduce.5.cloned.1.call-done = f32[1024,256]{1,0:T(8,128)} async-done(((f32[1024,256]{1,0:T(8,128)}), f32[1024,256]{1,0:T(8,128)}) %all-reduce.5.cloned.1.call-update) | async-done | bytes 1048592 | tf_op jit(solution)/shard_map/psum | solution.py:105
  756.4 2.3 copy.99
  (36 shorter events, 0.5 us)
Async XLA Ops:
  7.2 30.1 %copy-start = (bf16[1024,256]{1,0:T(8,128)(2,1)S(1)}, bf16[1024,256]{1,0:T(8,128)(2,1)}, u32[]{:S(2)}) copy-start(bf16[1024,256]{1,0:T(8,128)(2,1)} %param.5) | copy-start | bytes 1572868
  54.2 9.0 %copy-start.6 = (s32[16,8]{0,1:T(8,128)S(1)}, s32[16,8]{0,1:T(8,128)}, u32[]{:S(2)}) copy-start(s32[16,8]{0,1:T(8,128)} %param.9) | copy-start | bytes 1540
  54.2 191.6 %all-to-all-start.1 = ((bf16[128,128,256]{2,1,0:T(8,128)(2,1)}), bf16[128,128,256]{2,1,0:T(8,128)(2,1)}, u32[]{:S(2)}, u32[]{:S(2)}) async-start(bf16[128,128,256]{2,1,0:T(8,128)(2,1)} %copy.25), calls=%async_computation.1 | async-start | bytes 16777216 | tf_op jit(solution)/shard_map/all_to_all | solution.py:90
  62.0 246.7 %all-reduce.3.cloned.1.call-start = ((), (), s32[]{:S(2)}) async-start(), calls=%async_computation.3 | async-start | bytes 524288 | tf_op jit(solution)/shard_map/psum | solution.py:78
  63.1 693.3 %all-reduce.5.cloned.1.call-start = ((), (), s32[]{:S(2)}) async-start(), calls=%async_computation.4 | async-start | bytes 2097152 | tf_op jit(solution)/shard_map/psum | solution.py:105
  63.4 192.3 %copy-start.5 = (bf16[16,256]{1,0:T(8,128)(2,1)S(1)}, bf16[16,256]{1,0:T(8,128)(2,1)}, u32[]{:S(2)}) copy-start(bf16[16,256]{1,0:T(8,128)(2,1)} %param.6) | copy-start | bytes 24580
  255.7 5.8 copy-start.4
  255.7 5.8 copy-start.2
  315.5 4.8 copy-start.3
  315.5 5.4 slice-start
  315.6 5.9 slice-start.1
  337.1 421.6 %copy-start.1 = (bf16[1024,256]{1,0:T(8,128)(2,1)S(1)}, bf16[1024,256]{1,0:T(8,128)(2,1)}, u32[]{:S(2)}) copy-start(bf16[1024,256]{1,0:T(8,128)(2,1)} %param.5) | copy-start | bytes 1572868
Sparse Core Ops, SparseCore 0:
  68.8 239.8 all-reduce.2
  721.0 35.3 all-reduce.4
where the time goes:
time: 775 us; the launch traced here: 766 us
  blocking collectives  394 us (51%)
  waiting for transfers between devices  263 us (34%)
  matrix products  56.6 us (7%)
  local copies, waits for them, and re-layouts  26.5 us (3%)
  between operations  14.6 us (2%)
  starting transfers between devices  7.87 us (1%)
    all_to_all x1, blocking collectives, shards(): lax.all_to_all(partial_value.reshape(owners, TILE, factor_dim), ('user',...  367 us
    all_to_all x1, waiting for transfers between devices, shards(): lax.all_to_all(reply_tiles, ('user', 'item'), split_axis=0, concat_axis=0...  182 us
    psum x1, waiting for transfers between devices, shards(): gram_matrix = lax.psum(local_gram, ('user', 'item'))  44.8 us
    psum x1, waiting for transfers between devices, shards(): item_sums = lax.psum(owned_sums, 'rep')  35.6 us
    all_to_all x1, blocking collectives, shards(): lax.all_to_all(requests.reshape(owners), ('user', 'item'), split_axis=0,...  26.9 us
    dot_general x4, matrix products, against(): jnp.einsum('ur,ujr->uj', vectors, block, preferred_element_type=jnp.float32)  15.9 us
  transfers between devices with their start and end apart: 3, of which 3 were waited for; matrix products, arithmetic and copies ran while one was open for 3% of the time, Pallas kernels for 0%

commit v1 on v0

--- a/solution.py
+++ b/solution.py
@@ -8,6 +8,11 @@
 SLOTS_USER = 8
 ITERS = 2
 penalty = 1.0
+
+
+def add_all(x, name):
+    shards = lax.all_gather(x, name)
+    return jnp.sum(shards, axis=0)
 
 
 def absorb(tiles, gram_matrix, start_rows, strengths, user_slots):
@@ -75,7 +80,7 @@
     factor_dim = item_factors.shape[1]
     own_tiles = item_factors.reshape(tiles_here, TILE, factor_dim)
     local_gram = jnp.dot(item_factors.T, item_factors, preferred_element_type=jnp.float32)
-    gram_matrix = lax.psum(local_gram, ("user", "item"))
+    gram_matrix = add_all(local_gram, ("user", "item"))
     asked_tiles = lax.all_to_all(
         requests.reshape(owners), ("user", "item"), split_axis=0, concat_axis=0, tiled=True
     )

time: 775 us -> 858 us (1.11)
  waiting for transfers between devices: 263 us -> 326 us
  other arithmetic: 3.46 us -> 15.4 us
    all_to_all x1, waiting for transfers between devices: 182 us -> 246 us  [shards(): lax.all_to_all(reply_tiles, ('user', 'item'), split_axis=0, concat_axis=0...]
    all_gather x0 -> x1, waiting for transfers between devices: none -> 49.5 us  [add_all(): shards = lax.all_gather(x, name)]
    psum x1 -> x0, waiting for transfers between devices: 44.8 us -> none  [shards(): gram_matrix = lax.psum(local_gram, ('user', 'item'))]
    reduce_sum x0 -> x1, other arithmetic: none -> 12 us  [add_all(): return jnp.sum(shards, axis=0)]
  transfers between devices with their start and end apart: 3 -> 3, of which waited for: 3 -> 3; matrix products, arithmetic and copies ran while one was open for 3% -> 5% of each run, Pallas kernels for 0% -> 0%
where the time goes in v1:
time: 858 us; the launch traced here: 849 us
  blocking collectives  402 us (47%)
  waiting for transfers between devices  326 us (38%)
  matrix products  55.8 us (7%)
  local copies, waits for them, and re-layouts  27.8 us (3%)
  other arithmetic  15.4 us (2%)
  between operations  14.6 us (2%)
    all_to_all x1, blocking collectives, shards(): lax.all_to_all(partial_value.reshape(owners, TILE, factor_dim), ('user',...  375 us
    all_to_all x1, waiting for transfers between devices, shards(): lax.all_to_all(reply_tiles, ('user', 'item'), split_axis=0, concat_axis=0...  246 us
    all_gather x1, waiting for transfers between devices, add_all(): shards = lax.all_gather(x, name)  49.5 us
    psum x1, waiting for transfers between devices, shards(): item_sums = lax.psum(owned_sums, 'rep')  29.7 us
    all_to_all x1, blocking collectives, shards(): lax.all_to_all(requests.reshape(owners), ('user', 'item'), split_axis=0,...  26.9 us
  transfers between devices with their start and end apart: 3, of which 3 were waited for; matrix products, arithmetic and copies ran while one was open for 5% of the time, Pallas kernels for 0%

profile of v1, /device:TPU:1, one launch (start us, length us, event | category | flops | bytes accessed | tf_op | source)
XLA Modules:
  0.0 848.9 jit_solution(16510684455101726185)
XLA Ops:
  7.2 1.0 copy-done
  8.2 1.0 fusion.49
  9.3 0.8 copy.23
  10.0 26.9 %all_to_all.19 = s32[128,1,1]{2,1,0:T(1,128)S(1)} all-to-all(s32[128,1,1]{2,1,0:T(1,128)S(1)} %copy.23), channel_id=1, replica_groups=mesh['user'=32,'item'=4,'rep'=2] {'user','item'}, dimensions={0} | all-to-all | bytes 1024 | tf_op jit(solution)/shard_map/all_to_all | solution.py:84
  36.9 2.3 reduce
  39.3 5.6 convolution_convert_fusion
  44.9 11.4 %copy.25 = bf16[128,128,256]{2,1,0:T(8,128)(2,1)} copy(bf16[128,128,256]{2,0,1:T(8,128)(2,1)} %convolution_convert_fusion) | data formatting | bytes 16777216 | tf_op jit(solution)/shard_map/convert_element_type | solution.py:94
  56.2 7.8 all-to-all-start.1
  64.4 246.5 %all-to-all-done.1 = bf16[128,128,256]{2,1,0:T(8,128)(2,1)} async-done(((bf16[128,128,256]{2,1,0:T(8,128)(2,1)}), bf16[128,128,256]{2,1,0:T(8,128)(2,1)}, u32[]{:S(2)}, u32[]{:S(2)}) %all-to-all-start.1) | async-done | bytes 8388640 | tf_op jit(solution)/shard_map/all_to_all | solution.py:95
  310.9 10.4 %gather_fusion = bf16[128,128,256]{2,1,0:T(8,128)(2,1)} fusion(bf16[128,128,256]{2,1,0:T(8,128)(2,1)} %all-to-all-done.1, s32[1024]{0:T(1024)S(1)} %pad_clamp_fusion), kind=kCustom, calls=%fused_computation | custom fusion | bytes 16777728 | tf_op jit(solution)/shard_map/while/body/eval_jaxpr/gather | solution.py:27
  321.3 6.0 fusion.40
  327.3 1.2 fusion.23
  328.4 1.2 fusion.25
  329.6 49.5 %all-gather.3.cloned.1.call-done = f32[32768,256]{1,0:T(8,128)} async-done(((f32[256,256]{1,0:T(8,128)}), f32[32768,256]{1,0:T(8,128)}) %all-gather.3.cloned.1.call-update) | async-done | bytes 33554448 | tf_op jit(solution)/shard_map/all_gather | solution.py:14
  379.2 12.0 %reduce_sum.49 = f32[256,256]{1,0:T(8,128)S(1)} reduce(f32[128,256,256]{2,1,0:T(8,128)} %bitcast.102, f32[]{:T(128)} %constant.18.clone.1), dimensions={0}, to_apply=%region_0.0 | reduce | flops 8323072 | bytes 33816580 | tf_op jit(solution)/shard_map/reduce_sum | solution.py:15
  391.1 0.2 fusion.7
  391.4 5.6 fusion.38
  397.1 4.7 fusion.21
  401.8 0.3 multiply_reduce_fusion.1
  402.4 0.5 slice-done.1
  402.9 2.3 fusion.36
  405.2 1.2 fusion.19
  406.4 0.4 fusion.8
  406.7 0.7 convert_bitcast_fusion
  407.4 2.3 fusion.34
  409.8 0.6 convolution_convert_fusion.1
  410.3 8.1 fusion.9
  418.4 374.7 %all_to_all.20 = f32[128,128,256]{2,1,0:T(8,128)S(1)} all-to-all(f32[128,128,256]{2,1,0:T(8,128)} %fusion.9), channel_id=1, replica_groups=mesh['user'=32,'item'=4,'rep'=2] {'user','item'}, dimensions={0} | all-to-all | bytes 33554432 | tf_op jit(solution)/shard_map/all_to_all | solution.py:102
  793.1 15.2 %fusion = f32[8,128,256]{2,0,1:T(8,128)S(1)} fusion(f32[128,128,256]{2,1,0:T(8,128)S(1)} %all_to_all.20, s32[128]{0:T(128)S(1)} %reduce), kind=kOutput, calls=%fused_computation.1 | convolution fusion | flops 402654208 | bytes 17826304 | tf_op jit(solution)/shard_map/st,sjr->tjr/dot_general | solution.py:109
  808.3 1.3 copy.31
  809.6 29.7 %all-reduce.2.cloned.1.call-done = f32[1024,256]{1,0:T(8,128)} async-done(((f32[1024,256]{1,0:T(8,128)}), f32[1024,256]{1,0:T(8,128)}) %all-reduce.2.cloned.1.call-update) | async-done | bytes 1048592 | tf_op jit(solution)/shard_map/psum | solution.py:110
  839.3 2.3 copy.98
  (35 shorter events, 0.8 us)
Async XLA Ops:
  7.2 1.1 copy-start
  7.2 372.0 %all-gather.3.cloned.1.call-start = ((), (), s32[]{:S(2)}) async-start(), calls=%async_computation.4 | async-start | bytes 33816576 | tf_op jit(solution)/shard_map/all_gather | solution.py:14
  56.2 7.9 copy-start.5
  56.2 254.6 %all-to-all-start.1 = ((bf16[128,128,256]{2,1,0:T(8,128)(2,1)}), bf16[128,128,256]{2,1,0:T(8,128)(2,1)}, u32[]{:S(2)}, u32[]{:S(2)}) async-start(bf16[128,128,256]{2,1,0:T(8,128)(2,1)} %copy.25), calls=%async_computation.1 | async-start | bytes 16777216 | tf_op jit(solution)/shard_map/all_to_all | solution.py:95
  64.0 775.3 %all-reduce.2.cloned.1.call-start = ((), (), s32[]{:S(2)}) async-start(), calls=%async_computation.3 | async-start | bytes 2097152 | tf_op jit(solution)/shard_map/psum | solution.py:110
  64.4 256.9 %copy-start.4 = (bf16[16,256]{1,0:T(8,128)(2,1)S(1)}, bf16[16,256]{1,0:T(8,128)(2,1)}, u32[]{:S(2)}) copy-start(bf16[16,256]{1,0:T(8,128)(2,1)} %param.6) | copy-start | bytes 24580
  321.2 6.0 copy-start.3
  321.2 6.0 copy-start.2
  397.0 5.4 slice-start
  397.0 5.8 slice-start.1
  418.4 423.2 %copy-start.1 = (bf16[1024,256]{1,0:T(8,128)(2,1)S(1)}, bf16[1024,256]{1,0:T(8,128)(2,1)}, u32[]{:S(2)}) copy-start(bf16[1024,256]{1,0:T(8,128)(2,1)} %param.5) | copy-start | bytes 1572868
Sparse Core Ops, SparseCore 0:
  12.1 367.0 all-gather.2
  809.8 29.5 all-reduce.1
